TPU v7x, 1024 devices: a whole 4x8x16 slice. The times are simulated.
1024 devices in a mesh: expert: 64 (over x, y, core), mp: 16 (over z).
Axes of the slice: x: 4, y: 8, z: 16, core: 2. Of those that a mesh axis runs over, the one named last changes fastest.
Arguments:
- tokens: bfloat16 [1024, 2048], P('expert', 'mp'), may hold values from -6 to 6
- routes: int32 [1024, 6], P('expert'), may hold values from 0 to 63, all different within a row; in each aligned block of 16 rows (0 to 15, 16 to 31, ...) at most 2 rows name the same one
- probs: float32 [1024, 6], P('expert'), may hold values from 0.1 to 0.6
- w_gate: bfloat16 [64, 2048, 1408], P('expert', None, 'mp'), may hold values from -0.125 to 0.125
- w_up: bfloat16 [64, 2048, 1408], P('expert', None, 'mp'), may hold values from -0.125 to 0.125
- w_down: bfloat16 [64, 1408, 2048], P('expert', 'mp'), may hold values from -0.15625 to 0.15625
- grad_out: bfloat16 [1024, 2048], P('expert', 'mp'), may hold values from -1.5 to 1.5
Outputs:
- mixed: bfloat16 [1024, 2048], P('expert', 'mp')
- grad_tokens: bfloat16 [1024, 2048], P('expert', 'mp')
- grad_probs: float32 [1024, 6], P('expert')
- grad_gate: bfloat16 [64, 2048, 1408], P('expert', None, 'mp')
- grad_up: bfloat16 [64, 2048, 1408], P('expert', None, 'mp')
- grad_down: bfloat16 [64, 1408, 2048], P('expert', 'mp')
Inputs may be any that keep to these rules, and one draw needn't show every extreme that they name: `routes`: each row names 6 different experts. In each aligned block of 16 rows (one group) no expert is named by more than 2 rows, and every expert is named by some row.
All inputs are finite; a program needn't handle non-finite values.
Results may differ from a plain program's by a relative error of at most 0.029.
Values may be sent and summed in bfloat16 or wider, within the bound.
A program may use at most 32 MiB of HBM per device.

v0:
```python
import jax
import jax.numpy as jnp
from jax import lax
from jax.sharding import PartitionSpec as P


def forward_pass(slot_in, w_gate, w_up, w_down):
    local_exp = slot_in.shape[0]
    width = slot_in.shape[3]
    rows_in = slot_in.reshape(local_exp, -1, width)
    gate_act = jnp.einsum("jsd,jdf->jsf", rows_in, w_gate, preferred_element_type=jnp.float32)
    up_act = jnp.einsum("jsd,jdf->jsf", rows_in, w_up, preferred_element_type=jnp.float32)
    sigmoid_gate = jax.nn.sigmoid(gate_act)
    silu_gate = gate_act * sigmoid_gate
    hidden = (silu_gate * up_act).astype(jnp.bfloat16)
    out_part = jnp.einsum("jsf,jfd->jsd", hidden, w_down, preferred_element_type=jnp.float32)
    return (
        rows_in,
        gate_act,
        up_act,
        sigmoid_gate,
        silu_gate,
        hidden,
        out_part.reshape(slot_in.shape),
    )


def backward_pass(slot_grad, saved, w_gate, w_up, w_down):
    rows_in, gate_act, up_act, sigmoid_gate, silu_gate, hidden, out_part = saved
    local_exp = slot_grad.shape[0]
    width = slot_grad.shape[3]
    rows_grad = slot_grad.reshape(local_exp, -1, width)
    back_hidden = jnp.einsum("jsd,jfd->jsf", rows_grad, w_down, preferred_element_type=jnp.float32)
    up_grad = (back_hidden * silu_gate).astype(jnp.bfloat16)
    gate_grad = (
        back_hidden * up_act * sigmoid_gate * (1.0 + gate_act * (1.0 - sigmoid_gate))
    ).astype(jnp.bfloat16)
    both_grad = jnp.concatenate([gate_grad, up_grad], axis=2)
    both_weights = jnp.concatenate([w_gate, w_up], axis=2)
    back_part = jnp.einsum(
        "jsf,jdf->jsd", both_grad, both_weights, preferred_element_type=jnp.float32
    )
    grad_gate = jnp.einsum(
        "jsd,jsf->jdf", rows_in, gate_grad, preferred_element_type=jnp.float32
    ).astype(jnp.bfloat16)
    grad_up = jnp.einsum(
        "jsd,jsf->jdf", rows_in, up_grad, preferred_element_type=jnp.float32
    ).astype(jnp.bfloat16)
    grad_down = jnp.einsum(
        "jsf,jsd->jfd", hidden, rows_grad, preferred_element_type=jnp.float32
    ).astype(jnp.bfloat16)
    return (back_part.reshape(slot_grad.shape), grad_gate, grad_up, grad_down)


def local(tokens, routes, probs, w_gate, w_up, w_down, grad_out):
    highest = lax.Precision.HIGHEST
    group_rows = tokens.shape[0]
    choose_count = routes.shape[1]
    local_exp = w_gate.shape[0]
    groups = lax.axis_size("expert")
    experts = groups * local_exp
    capacity = max(2, (5 * choose_count * group_rows + 4 * experts - 1) // (4 * experts))
    matches = routes[:, :, None] == jnp.arange(experts, dtype=jnp.int32)[None, None, :]
    chosen = jnp.sum(matches.astype(jnp.int32), axis=1)
    weight = jnp.sum(
        jnp.where(matches, probs[:, :, None], jnp.zeros_like(probs[:, :, None])), axis=1
    )
    before = jnp.cumsum(chosen, axis=0) - chosen
    slot_ids = jnp.arange(capacity, dtype=jnp.int32)[None, None, :]
    one_hot = jnp.where(
        before[:, :, None] == slot_ids, chosen[:, :, None], jnp.zeros_like(chosen[:, :, None])
    )
    route_float = one_hot.astype(jnp.float32)
    dispatch = one_hot.astype(jnp.bfloat16)
    combine = route_float * weight[:, :, None]
    part_width = tokens.shape[1]
    send_in = jnp.einsum(
        "gec,gd->ecd", dispatch, tokens, preferred_element_type=jnp.float32
    ).astype(jnp.bfloat16)
    send_grad = jnp.einsum(
        "gec,gd->ecd", combine, grad_out.astype(jnp.float32), precision=highest
    ).astype(jnp.bfloat16)
    part_in, part_grad = (
        lax.all_to_all(
            send_in.reshape(experts, 1, capacity, part_width),
            "expert",
            split_axis=0,
            concat_axis=1,
            tiled=True,
        ),
        lax.all_to_all(
            send_grad.reshape(experts, 1, capacity, part_width),
            "expert",
            split_axis=0,
            concat_axis=1,
            tiled=True,
        ),
    )
    slot_in, slot_grad = (
        lax.all_gather(part_in, "mp", axis=3, tiled=True),
        lax.all_gather(part_grad, "mp", axis=3, tiled=True),
    )
    saved = forward_pass(slot_in, w_gate, w_up, w_down)
    back_part, grad_gate, grad_up, grad_down = backward_pass(slot_grad, saved, w_gate, w_up, w_down)
    out_sums, back_sums = (
        lax.psum_scatter(
            saved[6].astype(jnp.bfloat16), "mp", scatter_dimension=3, tiled=True
        ).astype(jnp.float32),
        lax.psum_scatter(
            back_part.astype(jnp.bfloat16), "mp", scatter_dimension=3, tiled=True
        ).astype(jnp.float32),
    )
    out_home, back_home = (
        lax.all_to_all(
            out_sums.astype(jnp.bfloat16), "expert", split_axis=1, concat_axis=0, tiled=True
        ),
        lax.all_to_all(
            back_sums.astype(jnp.bfloat16), "expert", split_axis=1, concat_axis=0, tiled=True
        ),
    )
    home_width = out_home.shape[3]
    out_float = out_home.reshape(experts, capacity, home_width).astype(jnp.float32)
    back_float = back_home.reshape(experts, capacity, home_width).astype(jnp.float32)
    mixed = jnp.einsum("gec,ecd->gd", combine, out_float, precision=highest).astype(jnp.bfloat16)
    grad_tokens = jnp.einsum("gec,ecd->gd", route_float, back_float, precision=highest).astype(
        jnp.bfloat16
    )
    scores = jnp.einsum("ecd,gd->gec", out_float, grad_out.astype(jnp.float32), precision=highest)
    per_expert = jnp.sum(route_float * scores, axis=2)
    partial_probs = jnp.sum(
        jnp.where(matches, per_expert[:, None, :], jnp.zeros_like(per_expert[:, None, :])), axis=2
    )
    grad_probs = lax.psum(partial_probs, "mp")
    return (mixed, grad_tokens, grad_probs, grad_gate, grad_up, grad_down)


def solution(mesh):
    placed = (
        P("expert", "mp"),
        P("expert", None),
        P("expert", None),
        P("expert", None, "mp"),
        P("expert", None, "mp"),
        P("expert", "mp", None),
        P("expert", "mp"),
    )
    return jax.shard_map(
        local,
        mesh=mesh,
        in_specs=placed,
        out_specs=(
            P("expert", "mp"),
            P("expert", "mp"),
            P("expert", None),
            P("expert", None, "mp"),
            P("expert", None, "mp"),
            P("expert", "mp", None),
        ),
        check_vma=False,
    )
```

profile of v0, /device:TPU:1, one launch (start us, length us, event | category | flops | bytes accessed | tf_op | source)
XLA Modules:
  0.0 300.8 jit_solution(10998712120514412938)
XLA Ops:
  7.2 0.0 copy-start
  7.2 0.0 reduce-scatter.7.cloned.1.call-start
  7.2 0.9 convert_reduce_fusion
  8.1 0.9 fusion.5
  9.1 26.8 %all_to_all.42 = bf16[64,1,2,128]{3,2,1,0:T(2,128)(2,1)S(1)} all-to-all(bf16[64,1,2,128]{3,2,1,0:T(2,128)(2,1)S(1)} %copy.42), channel_id=1, replica_groups=mesh['expert'=64,'mp'=16] {'expert'}, dimensions={0} | all-to-all | bytes 65536 | tf_op jit(solution)/shard_map/all_to_all | solution.py:84
  35.8 32.3 %all-gather = bf16[64,1,2,2048]{3,2,1,0:T(2,128)(2,1)S(1)} all-gather(bf16[64,1,2,128]{3,2,1,0:T(2,128)(2,1)S(1)} %all_to_all.42), channel_id=2, replica_groups=mesh['expert'=64,'mp'=16] {'mp'}, dimensions={3}, use_global_device_ids=true | all-gather | bytes 557056 | tf_op jit(solution)/shard_map/all_gather | solution.py:100
  68.2 0.2 reshape.136
  68.4 0.3 fusion.18
  68.7 0.5 copy-done.2
  69.1 0.3 multiply_convert_fusion.2
  69.5 0.1 copy.43
  69.6 0.3 fusion
  69.9 0.8 copy.54
  70.7 0.0 copy-start.4
  70.7 0.0 copy-start.6
  70.7 1.3 reshape.155
  72.0 0.0 reduce-scatter.7.cloned.1.call-update
  72.0 0.0 reduce-scatter.9.cloned.1.call-start
  72.0 56.2 %reduce-scatter.7.cloned.1.call-done = bf16[128,128]{1,0:T(8,128)(2,1)} async-done(((bf16[2048,128]{1,0:T(8,128)(2,1)}), bf16[128,128]{1,0:T(8,128)(2,1)}) %reduce-scatter.7.cloned.1.call-update) | async-done | bytes 32784
  128.2 0.8 reshape.156
  129.1 0.1 copy.45
  129.2 29.9 %all_to_all.43 = bf16[1,64,2,128]{3,2,0,1:T(2,128)(2,1)S(1)} all-to-all(bf16[1,64,2,128]{3,2,0,1:T(2,128)(2,1)S(1)} %copy.45), channel_id=1, replica_groups=mesh['expert'=64,'mp'=16] {'expert'}, dimensions={1} | all-to-all | bytes 65536 | tf_op jit(solution)/shard_map/all_to_all | solution.py:114
  159.1 0.1 fusion.8
  159.3 0.0 copy-done.6
  159.3 0.2 select_reduce_fusion
  159.5 0.2 fusion.6
  159.8 13.3 %all_to_all.44 = bf16[64,1,2,128]{3,2,1,0:T(2,128)(2,1)S(1)} all-to-all(bf16[64,1,2,128]{3,2,1,0:T(2,128)(2,1)S(1)} %copy.47), channel_id=1, replica_groups=mesh['expert'=64,'mp'=16] {'expert'}, dimensions={0} | all-to-all | bytes 65536 | tf_op jit(solution)/shard_map/all_to_all | solution.py:91
  173.1 23.4 %all-gather.1 = bf16[64,1,2,2048]{3,2,1,0:T(2,128)(2,1)S(1)} all-gather(bf16[64,1,2,128]{3,2,1,0:T(2,128)(2,1)S(1)} %all_to_all.44), channel_id=3, replica_groups=mesh['expert'=64,'mp'=16] {'mp'}, dimensions={3}, use_global_device_ids=true | all-gather | bytes 557056 | tf_op jit(solution)/shard_map/all_gather | solution.py:101
  196.4 0.2 reshape.142
  196.6 0.3 multiply_convert_fusion.1
  196.9 0.1 copy.48
  197.1 0.1 copy.49
  197.2 0.2 copy-done.3
  197.4 0.4 fusion.1
  197.8 0.8 copy.56
  198.5 1.3 reshape.157
  199.8 0.0 reduce-scatter.9.cloned.1.call-update
  199.8 22.6 %psum.7 = f32[16,6]{0,1:T(8,128)} all-reduce(f32[16,6]{0,1:T(8,128)S(1)} %get-tuple-element.6), channel_id=1, replica_groups=mesh['expert'=64,'mp'=16] {'mp'}, use_global_device_ids=true, to_apply=%region_7.8 | all-reduce | flops 96 | bytes 768 | tf_op jit(solution)/shard_map/psum | solution.py:133
  222.5 0.8 fusion.9
  223.3 1.0 fusion.4
  224.2 1.0 fusion.3
  225.2 36.4 %reduce-scatter.9.cloned.1.call-done = bf16[128,128]{1,0:T(8,128)(2,1)} async-done(((bf16[2048,128]{1,0:T(8,128)(2,1)}), bf16[128,128]{1,0:T(8,128)(2,1)}) %reduce-scatter.9.cloned.1.call-update) | async-done | bytes 32784
  261.6 0.8 reshape.158
  262.4 0.7 copy.52
  263.1 20.8 %all-to-all-start.3 = ((bf16[1,64,2,128]{3,2,0,1:T(2,128)(2,1)}), bf16[1,64,2,128]{3,2,0,1:T(2,128)(2,1)S(1)}, u32[]{:S(2)}, u32[]{:S(2)}) async-start(bf16[1,64,2,128]{3,2,0,1:T(2,128)(2,1)} %copy.52), calls=%async_computation.3 | async-start | bytes 65536 | tf_op jit(solution)/shard_map/all_to_all | solution.py:117
  283.9 1.0 fusion.2
  284.9 8.3 %all-to-all-done.3 = bf16[1,64,2,128]{3,2,0,1:T(2,128)(2,1)S(1)} async-done(((bf16[1,64,2,128]{3,2,0,1:T(2,128)(2,1)}), bf16[1,64,2,128]{3,2,0,1:T(2,128)(2,1)S(1)}, u32[]{:S(2)}, u32[]{:S(2)}) %all-to-all-start.3) | async-done | bytes 32800 | tf_op jit(solution)/shard_map/all_to_all | solution.py:117
  293.2 0.8 fusion.10
  (14 shorter events, 0.1 us)
Async XLA Ops:
  7.2 62.4 %copy-start = (bf16[1,88,2048]{2,1,0:T(8,128)(2,1)S(1)}, bf16[1,88,2048]{2,1,0:T(8,128)(2,1)}, u32[]{:S(2)}) copy-start(bf16[1,88,2048]{2,1,0:T(8,128)(2,1)} %param.12) | copy-start | bytes 1081348
  7.2 61.2 %copy-start.1 = (bf16[1,2048,88]{1,2,0:T(8,128)(2,1)S(1)}, bf16[1,2048,88]{1,2,0:T(8,128)(2,1)}, u32[]{:S(2)}) copy-start(bf16[1,2048,88]{1,2,0:T(8,128)(2,1)} %param.10) | copy-start | bytes 1081348
  7.2 121.0 %reduce-scatter.7.cloned.1.call-start = ((), (), s32[]{:S(2)}) async-start(), calls=%async_computation.6 | async-start | bytes 557056
  68.1 1.0 copy-start.2
  70.6 88.5 %copy-start.5 = (bf16[16,128]{1,0:T(8,128)(2,1)S(1)}, bf16[16,128]{1,0:T(8,128)(2,1)}, u32[]{:S(2)}) copy-start(bf16[16,128]{1,0:T(8,128)(2,1)} %param.13) | copy-start | bytes 12292
  70.7 88.6 %copy-start.4 = (s32[16,6]{0,1:T(8,128)S(1)}, s32[16,6]{0,1:T(8,128)}, u32[]{:S(2)}) copy-start(s32[16,6]{0,1:T(8,128)} %param.8) | copy-start | bytes 1156
  70.7 88.6 %copy-start.6 = (f32[16,6]{0,1:T(8,128)S(1)}, f32[16,6]{0,1:T(8,128)}, u32[]{:S(2)}) copy-start(f32[16,6]{0,1:T(8,128)} %param.9) | copy-start | bytes 1156
  72.0 189.6 %reduce-scatter.9.cloned.1.call-start = ((), (), s32[]{:S(2)}) async-start(), calls=%async_computation.7 | async-start | bytes 557056
  196.4 1.0 copy-start.3
  263.1 30.1 %all-to-all-start.3 = ((bf16[1,64,2,128]{3,2,0,1:T(2,128)(2,1)}), bf16[1,64,2,128]{3,2,0,1:T(2,128)(2,1)S(1)}, u32[]{:S(2)}, u32[]{:S(2)}) async-start(bf16[1,64,2,128]{3,2,0,1:T(2,128)(2,1)} %copy.52), calls=%async_computation.3 | async-start | bytes 65536 | tf_op jit(solution)/shard_map/all_to_all | solution.py:117
Sparse Core Ops, SparseCore 0:
  72.1 56.0 reduce-scatter.6
  200.0 61.5 reduce-scatter.8
where the time goes:
time: 301 us
  blocking collectives  148 us (49%)
  waiting for transfers between devices  101 us (34%)
  starting transfers between devices  20.8 us (7%)
  between operations  14.3 us (5%)
  local copies, waits for them, and re-layouts  8.14 us (3%)
  matrix products  7.38 us (2%)
    unnamed x4, waiting for transfers between devices  92.6 us
    all_gather x1, blocking collectives, local(): lax.all_gather(part_in, 'mp', axis=3, tiled=True)  32.3 us
    all_to_all x1, blocking collectives, local(): lax.all_to_all(out_sums.astype(jnp.bfloat16), 'expert', split_axis=1, con...  29.9 us
    all_to_all x1, blocking collectives, local(): lax.all_to_all(send_in.reshape(experts, 1, capacity, part_width), 'expert...  26.8 us
    all_gather x1, blocking collectives, local(): lax.all_gather(part_grad, 'mp', axis=3, tiled=True)  23.4 us
    psum x1, blocking collectives, local(): grad_probs = lax.psum(partial_probs, 'mp')  22.6 us
    all_to_all x1, starting transfers between devices, local(): lax.all_to_all(back_sums.astype(jnp.bfloat16), 'expert', split_axis=1, co...  20.8 us
    all_to_all x1, blocking collectives, local(): lax.all_to_all(send_grad.reshape(experts, 1, capacity, part_width), 'expe...  13.3 us
  transfers between devices with their start and end apart: 3, of which 3 were waited for; matrix products, arithmetic and copies ran while one was open for 1% of the time, Pallas kernels for 0%

commit v1 on v0

v1 whole, which is shorter than its diff:
```python
import functools

import jax
import jax.numpy as jnp
from jax import lax
from jax.experimental import pallas as pl
from jax.experimental.pallas import tpu as pltpu
from jax.sharding import PartitionSpec as P

MESH = pl.DeviceIdType.MESH
BF = jnp.bfloat16
F32 = jnp.float32


def dot(a, b):
    return jnp.dot(a, b, preferred_element_type=F32)


def dot_nt(a, b):
    return lax.dot_general(a, b, (((1,), (1,)), ((), ())), preferred_element_type=F32)


def kernel(
    ny, nxc, nz,
    tok, gout, rt, pt, wg_h, wu_h, wd_h,
    mixed, gtok, gprob, ogg, ogu, ogd,
    wg, wu, wd, disp, disp_t, s_buf, r1, b_buf, xg, acc, h_t, h_r, part, tx, rx, own,
    sc_own, sc_all, o_buf, q1, q2, home, gw,
    w_sem, ow_sem, a1_send, a1_recv, a2_send, a2_recv, ag_send, ag_recv, rs_send, rs_recv,
    sc_send, sc_recv, b1_send, b1_recv, b2_send, b2_recv,
):
    e = lax.axis_index("expert")
    m = lax.axis_index("mp")
    x_me = e // (2 * ny)
    y_me = (e // 2) % ny
    xc_me = x_me * 2 + e % 2
    half = nz // 2
    rows = ny * nxc * 2
    nt = tok.shape[0]
    topk = rt.shape[0]

    def y_peer(d):
        y2 = lax.rem(y_me + d, ny)
        return y2, (x_me * ny + y2) * 2 + e % 2

    def xc_peer(d):
        xc2 = lax.rem(xc_me + d, nxc)
        return xc2, ((xc2 // 2) * ny + y_me) * 2 + xc2 % 2

    def z_at(d):
        return lax.rem(m + d + 2 * nz, nz)

    right, left = z_at(1), z_at(-1)

    loads = [
        pltpu.make_async_copy(src, dst, w_sem.at[i])
        for i, (src, dst) in enumerate(((wg_h, wg), (wu_h, wu), (wd_h, wd)))
    ]
    for c in loads:
        c.start()

    barrier = pltpu.get_barrier_semaphore()
    for d in range(1, ny):
        pl.semaphore_signal(barrier, inc=1, device_id={"expert": y_peer(d)[1]}, device_id_type=MESH)
    for d in range(1, nxc):
        pl.semaphore_signal(barrier, inc=1, device_id={"expert": xc_peer(d)[1]}, device_id_type=MESH)
    for d in range(1, nz):
        pl.semaphore_signal(barrier, inc=1, device_id={"mp": z_at(d)}, device_id_type=MESH)

    r = lax.broadcasted_iota(jnp.int32, (rows, nt), 0)
    sy = nxc * 2
    y_r = r // sy
    xc_r = (r % sy) // 2
    slot_r = r % 2
    e_r = (xc_r // 2) * (2 * ny) + y_r * 2 + xc_r % 2
    chosen = jnp.zeros((rows, nt), F32)
    weight = jnp.zeros((rows, nt), F32)
    for k in range(topk):
        hit = rt[k : k + 1, :] == e_r
        chosen = jnp.where(hit, 1.0, chosen)
        weight = jnp.where(hit, pt[k : k + 1, :], weight)
    t0 = lax.broadcasted_iota(jnp.int32, (nt, nt), 0)
    t1 = lax.broadcasted_iota(jnp.int32, (nt, nt), 1)
    earlier = jnp.where(t0 < t1, 1.0, 0.0).astype(BF)
    before = dot(chosen.astype(BF), earlier)
    d_f = jnp.where(before == slot_r.astype(F32), chosen, 0.0)
    d_w = d_f * weight
    disp[...] = d_f
    d_b = d_f.astype(BF)
    w_row = jnp.sum(d_w, axis=1, keepdims=True)
    s_buf[0] = dot(d_b, tok[...]).astype(BF)
    s_buf[1] = (dot(d_b, gout[...]) * w_row).astype(BF)

    pl.semaphore_wait(barrier, (ny - 1) + (nxc - 1) + (nz - 1))

    def chunk(i, n):
        return pl.ds(pl.multiple_of(i * n, n), n)

    def send_y(src, dst, ss, rs):
        copies = []
        for d in range(1, ny):
            y2, peer = y_peer(d)
            c = pltpu.make_async_remote_copy(
                src_ref=src.at[:, chunk(y2, sy), :], dst_ref=dst.at[:, chunk(y_me, sy), :],
                send_sem=ss.at[d], recv_sem=rs.at[d], device_id={"expert": peer}, device_id_type=MESH)
            c.start()
            copies.append(c)
        dst[:, chunk(y_me, sy), :] = src[:, chunk(y_me, sy), :]
        return copies

    sx = ny * 2

    def send_xc(src, dst, ss, rs):
        copies = []
        for d in range(1, nxc):
            xc2, peer = xc_peer(d)
            c = pltpu.make_async_remote_copy(
                src_ref=src.at[:, chunk(xc2, sx), :], dst_ref=dst.at[:, chunk(xc_me, sx), :],
                send_sem=ss.at[d], recv_sem=rs.at[d], device_id={"expert": peer}, device_id_type=MESH)
            c.start()
            copies.append(c)
        dst[:, chunk(xc_me, sx), :] = src[:, chunk(xc_me, sx), :]
        return copies

    pending = []

    a1 = send_y(s_buf, r1, a1_send, a1_recv)
    pending += a1

    t_f = jnp.transpose(d_f)
    t_w = jnp.transpose(d_w)
    t_hi = t_w.astype(BF)
    disp_t[0] = t_hi
    disp_t[1] = (t_w - t_hi.astype(F32)).astype(BF)
    disp_t[2] = t_f.astype(BF)
    p0 = lax.broadcasted_iota(jnp.int32, (rows, rows), 0)
    p1 = lax.broadcasted_iota(jnp.int32, (rows, rows), 1)
    source = ((p0 % sx) // 2) * sy + (p0 // sx) * 2 + p0 % 2
    swap = jnp.where(p1 == source, 1.0, 0.0).astype(BF)
    for a in range(3):
        acc[a] = jnp.zeros(acc.shape[1:], F32)

    for c in a1:
        c.wait_recv()
    for a in range(2):
        b_buf[a] = dot(swap, r1[a]).astype(BF)

    a2 = send_xc(b_buf, xg.at[m], a2_send, a2_recv)
    pending += a2
    for c in loads:
        c.wait()
    for c in a2:
        c.wait_recv()

    def hop(way, a, s):
        to, sign = ((right, -1), (left, 1))[way]
        blk = z_at(sign * (s - 1))
        return pltpu.make_async_remote_copy(
            src_ref=xg.at[blk, a], dst_ref=xg.at[blk, a],
            send_sem=ag_send.at[way, a, s], recv_sem=ag_recv.at[way, a, s],
            device_id={"mp": to}, device_id_type=MESH)

    def cols(blk):
        return pl.ds(pl.multiple_of(blk * 128, 128), 128)

    def use(blk, a):
        v = xg[blk, a]
        if a == 0:
            acc[0] += dot_nt(wg[:, cols(blk)], v)
            acc[1] += dot_nt(wu[:, cols(blk)], v)
        else:
            acc[2] += dot_nt(wd[:, cols(blk)], v)

    def last(way, a):
        return half if way == a else half - 1

    for a in range(2):
        for way in range(2):
            hop(way, a, 1).start()
    for a in range(2):
        use(m, a)

    def ag_step(s, full):
        for a in range(2):
            for way in range(2):
                hop(way, a, s).wait_recv()
                if full or s < last(way, a):
                    hop(way, a, s + 1).start()
        for a in range(2):
            for way in range(2):
                use(z_at((-1, 1)[way] * s), a)

    def ag_body(s, carry):
        ag_step(s, True)
        return carry

    lax.fori_loop(1, half - 1, ag_body, 0)
    ag_step(half - 1, False)
    for a in range(2):
        hop(a, a, half).wait_recv()
    for a in range(2):
        use(z_at(half), a)

    gate, up, back = acc[0], acc[1], acc[2]
    sig = jax.nn.sigmoid(gate)
    silu = gate * sig
    hid = silu * up
    u_g = back * silu
    g_g = back * up * sig * (1.0 + gate * (1.0 - sig))
    sc_own[...] = jnp.broadcast_to(jnp.sum(hid * back, axis=0, keepdims=True), sc_own.shape)
    scores = []
    for d in range(1, nz):
        c = pltpu.make_async_remote_copy(
            src_ref=sc_own, dst_ref=sc_all.at[m], send_sem=sc_send.at[d], recv_sem=sc_recv.at[d],
            device_id={"mp": z_at(d)}, device_id_type=MESH)
        c.start()
        scores.append(c)
    pending += scores
    for i, v in enumerate((hid, g_g, u_g)):
        h_r[i] = jnp.transpose(v).astype(BF)
        h_t[i] = v.astype(BF)

    def blk_at(way, a, s):
        n = last(way, a)
        return z_at(n + 1 - s) if way == 0 else z_at(s - n - 1)

    def partial(a, blk):
        if a == 0:
            return dot(h_r[0], wd[:, cols(blk)])
        return dot(h_r[1], wg[:, cols(blk)]) + dot(h_r[2], wu[:, cols(blk)])

    def turn(way, a, s):
        return pltpu.make_async_remote_copy(
            src_ref=tx.at[way, a, s], dst_ref=rx.at[way, a, s],
            send_sem=rs_send.at[way, a, s], recv_sem=rs_recv.at[way, a, s],
            device_id={"mp": (right, left)[way]}, device_id_type=MESH)

    def weights_of(blk):
        x_v, g_v = xg[blk, 0], xg[blk, 1]
        gw[0, :, cols(blk)] = dot(h_t[1], x_v).astype(BF)
        gw[1, :, cols(blk)] = dot(h_t[2], x_v).astype(BF)
        gw[2, :, cols(blk)] = dot(h_t[0], g_v).astype(BF)

    for a in range(2):
        for way in range(2):
            tx[way, a, 1] = partial(a, blk_at(way, a, 1)).astype(BF)
            turn(way, a, 1).start()
    for a in range(2):
        for way in range(2):
            part[way, a] = partial(a, blk_at(way, a, 2))
    weights_of(0)
    weights_of(1)

    def rs_step(s, full):
        for a in range(2):
            for way in range(2):
                if full or s <= last(way, a):
                    turn(way, a, s - 1).wait_recv()
                    tx[way, a, s] = (part[way, a] + rx[way, a, s - 1].astype(F32)).astype(BF)
                    turn(way, a, s).start()
        for a in range(2):
            for way in range(2):
                if full or s + 1 <= last(way, a):
                    part[way, a] = partial(a, blk_at(way, a, s + 1))
        weights_of(2 * s - 2)
        weights_of(2 * s - 1)

    def rs_body(s, carry):
        rs_step(s, True)
        return carry

    lax.fori_loop(2, half - 1, rs_body, 0)
    for s in range(max(2, half - 1), half + 1):
        rs_step(s, False)
    out_w = [pltpu.make_async_copy(gw.at[i], ref, ow_sem.at[i]) for i, ref in enumerate((ogg, ogu, ogd))]
    for c in out_w:
        c.start()
    for a in range(2):
        own[a] = partial(a, m)

    sc_all[m] = sc_own[...]
    for c in scores:
        c.wait_recv()
    sc = jnp.sum(sc_all[...], axis=0)[0:1, :]
    sc_col = jnp.sum(jnp.where(p0 == p1, jnp.broadcast_to(sc, (rows, rows)), 0.0), axis=1, keepdims=True)
    hi = sc_col.astype(BF).astype(F32)
    lane = lax.broadcasted_iota(jnp.int32, (rows, 128), 1)
    o_buf[2] = jnp.where(lane == 0, hi, jnp.where(lane == 1, sc_col - hi, 0.0)).astype(BF)

    for a in range(2):
        total = own[a]
        for way in (1 - a, a):
            n = last(way, a)
            turn(way, a, n).wait_recv()
            total = total + rx[way, a, n].astype(F32)
        o_buf[a] = total.astype(BF)

    b1 = send_xc(o_buf, q1, b1_send, b1_recv)
    pending += b1
    for c in b1:
        c.wait_recv()
    for a in range(3):
        q2[a] = dot(swap, q1[a]).astype(BF)
    b2 = send_y(q2, home, b2_send, b2_recv)
    pending += b2

    for c in pending:
        c.wait_send()
    for s in range(1, half + 1):
        for a in range(2):
            for way in range(2):
                if s <= last(way, a):
                    hop(way, a, s).wait_send()
                    turn(way, a, s).wait_send()
    for c in out_w:
        c.wait()
    for c in b2:
        c.wait_recv()

    mixed[...] = (dot(disp_t[0], home[0]) + dot(disp_t[1], home[0])).astype(BF)
    gtok[...] = dot(disp_t[2], home[1]).astype(BF)
    col = home[2].astype(F32)
    col = disp[...] * (col[:, 0:1] + col[:, 1:2])
    for k in range(topk):
        picked = jnp.sum(jnp.where(rt[k : k + 1, :] == e_r, col, 0.0), axis=0, keepdims=True)
        gprob[k : k + 1, :] = picked / pt[k : k + 1, :]


def local(ny, nxc, nz, tokens, routes, probs, w_gate, w_up, w_down, grad_out):
    nt, width = tokens.shape
    topk = routes.shape[1]
    d, f = w_gate.shape[1:]
    rows = ny * nxc * 2
    half = nz // 2
    vmem = pl.BlockSpec(memory_space=pltpu.VMEM)
    hbm = pl.BlockSpec(memory_space=pl.ANY)
    dma = pltpu.SemaphoreType.DMA
    V = pltpu.VMEM
    outs = pl.pallas_call(
        functools.partial(kernel, ny, nxc, nz),
        out_shape=(
            jax.ShapeDtypeStruct((nt, width), BF),
            jax.ShapeDtypeStruct((nt, width), BF),
            jax.ShapeDtypeStruct((topk, nt), F32),
            jax.ShapeDtypeStruct((f, d), BF),
            jax.ShapeDtypeStruct((f, d), BF),
            jax.ShapeDtypeStruct((f, d), BF),
        ),
        in_specs=[vmem] * 4 + [hbm] * 3,
        out_specs=(vmem, vmem, vmem, hbm, hbm, hbm),
        scratch_shapes=[
            V((f, d), BF), V((f, d), BF), V((f, d), BF),
            V((rows, nt), F32), V((3, nt, rows), BF),
            V((2, rows, width), BF), V((2, rows, width), BF), V((2, rows, width), BF),
            V((nz, 2, rows, width), BF),
            V((3, f, rows), F32), V((3, f, rows), BF), V((3, rows, f), BF),
            V((2, 2, rows, width), F32),
            V((2, 2, half + 1, rows, width), BF), V((2, 2, half + 1, rows, width), BF),
            V((2, rows, width), F32),
            V((8, rows), F32), V((nz, 8, rows), F32),
            V((3, rows, width), BF), V((3, rows, width), BF), V((3, rows, width), BF), V((3, rows, width), BF),
            V((3, f, d), BF),
            dma((3,)), dma((3,)),
            dma((ny,)), dma((ny,)), dma((nxc,)), dma((nxc,)),
            dma((2, 2, half + 1)), dma((2, 2, half + 1)), dma((2, 2, half + 1)), dma((2, 2, half + 1)),
            dma((nz,)), dma((nz,)),
            dma((nxc,)), dma((nxc,)), dma((ny,)), dma((ny,)),
        ],
        compiler_params=pltpu.CompilerParams(
            collective_id=0, has_side_effects=True, vmem_limit_bytes=24 * 1024 * 1024
        ),
    )(
        tokens, grad_out, routes.T, probs.T,
        jnp.swapaxes(w_gate, 1, 2).reshape(f, d), jnp.swapaxes(w_up, 1, 2).reshape(f, d), w_down.reshape(f, d),
    )
    mixed, gtok, gprob, gg, gu, gd = outs
    return (
        mixed, gtok, gprob.T,
        jnp.swapaxes(gg.reshape(1, f, d), 1, 2), jnp.swapaxes(gu.reshape(1, f, d), 1, 2), gd.reshape(1, f, d),
    )


def solution(mesh):
    n_exp, nz = mesh.shape["expert"], mesh.shape["mp"]
    ny = 8 if n_exp == 64 else 2
    nxc = n_exp // ny
    placed = (
        P("expert", "mp"),
        P("expert", None),
        P("expert", None),
        P("expert", None, "mp"),
        P("expert", None, "mp"),
        P("expert", "mp", None),
        P("expert", "mp"),
    )
    return jax.shard_map(
        functools.partial(local, ny, nxc, nz),
        mesh=mesh,
        in_specs=placed,
        out_specs=(
            P("expert", "mp"),
            P("expert", "mp"),
            P("expert", None),
            P("expert", None, "mp"),
            P("expert", None, "mp"),
            P("expert", "mp", None),
        ),
        check_vma=False,
    )
```

time: 301 us -> 108 us (0.36)
  blocking collectives: 148 us -> 0 us
  waiting for transfers between devices: 101 us -> 0 us
  Pallas kernels: 0 us -> 98.2 us
  starting transfers between devices: 20.8 us -> 0 us
  between operations: 14.3 us -> 0.67 us
  matrix products: 7.38 us -> 0 us
    pallas_call x0 -> x1, Pallas kernels: none -> 98.2 us  [local(): pl.pallas_call(functools.partial(kernel, ny, nxc, nz), out_shape=(jax.Sha...]
    unnamed x4 -> x0, waiting for transfers between devices: 92.6 us -> none
    all_to_all x3 -> x0, blocking collectives: 70 us -> none  [the longest x1 29.9 us: local(): lax.all_to_all(out_sums.astype(jnp.bfloat16), 'expert', split_axis=1, con...]
    all_gather x2 -> x0, blocking collectives: 55.7 us -> none  [the longest x1 32.3 us: local(): lax.all_gather(part_in, 'mp', axis=3, tiled=True)]
    psum x1 -> x0, blocking collectives: 22.6 us -> none  [local(): grad_probs = lax.psum(partial_probs, 'mp')]
    all_to_all x1 -> x0, starting transfers between devices: 20.8 us -> none  [local(): lax.all_to_all(back_sums.astype(jnp.bfloat16), 'expert', split_axis=1, co...]
    all_to_all x1 -> x0, waiting for transfers between devices: 8.3 us -> none  [local(): lax.all_to_all(back_sums.astype(jnp.bfloat16), 'expert', split_axis=1, co...]
    dot_general x13 -> x0, matrix products: 7.38 us -> none  [the longest x1 0.99 us: backward_pass(): jnp.einsum('jsd,jsf->jdf', rows_in, gate_grad, preferred_element_type=jnp...]
  transfers between devices with their start and end apart: 3 -> 0, of which waited for: 3 -> 0; matrix products, arithmetic and copies ran while one was open for 1% -> 0% of each run, Pallas kernels for 0% -> 0%
where the time goes in v1:
time: 108 us
  Pallas kernels  98.2 us (91%)
  local copies, waits for them, and re-layouts  8.99 us (8%)
    pallas_call x1, Pallas kernels, local(): pl.pallas_call(functools.partial(kernel, ny, nxc, nz), out_shape=(jax.Sha...  98.2 us
    unnamed x20, local copies, waits for them, and re-layouts  8.99 us

profile of v1, /device:TPU:1, one launch (start us, length us, event | category | flops | bytes accessed | tf_op | source)
XLA Modules:
  0.0 107.9 jit_solution(6676671377518282632)
XLA Ops:
  0.6 0.0 copy-start.4
  0.6 0.0 copy-start.3
  0.7 0.7 copy-done.4
  1.3 0.0 copy-done.3
  1.3 0.0 copy-start
  1.3 1.0 copy-done
  2.3 0.0 copy-start.1
  2.3 1.0 copy-done.1
  3.3 0.0 copy-start.2
  3.3 1.0 copy-done.2
  4.3 0.0 copy-start.5
  4.3 0.7 copy-done.5
  5.0 0.0 copy-start.6
  5.0 0.7 copy-done.6
  5.7 98.2 %shard_map.118 = (bf16[16,128]{1,0:T(8,128)(2,1)S(1)}, bf16[16,128]{1,0:T(8,128)(2,1)S(1)}, f32[6,16]{1,0:T(8,128)S(1)}, bf16[88,2048]{1,0:T(8,128)(2,1)S(1)}, b...) custom-call(bf16[16,128]{1,0:T(8,128)(2,1)S(1)} %copy-done.3, bf16[16,128]{1,0:T(8,128)(2,1)S(1)} %copy-done.4, ...), custom_call_target="tpu_custom_call" | custom-call | tf_op jit(solution)/shard_map/pallas_call | solution.py:339
  103.9 0.6 copy.19
  104.5 0.6 copy.20
  105.1 0.6 copy.21
  105.7 0.7 copy.22
  106.4 0.7 copy.23
  107.1 0.7 copy.24
Async XLA Ops:
  0.6 0.7 copy-start.4
  0.6 0.7 copy-start.3
  1.3 1.0 copy-start
  2.3 1.0 copy-start.1
  3.3 1.0 copy-start.2
  4.3 0.7 copy-start.5
  5.0 0.7 copy-start.6

commit v2 on v1

--- a/solution.py
+++ b/solution.py
@@ -22,11 +22,11 @@
 
 def kernel(
     ny, nxc, nz,
-    tok, gout, rt, pt, wg_h, wu_h, wd_h,
-    mixed, gtok, gprob, ogg, ogu, ogd,
-    wg, wu, wd, disp, disp_t, s_buf, r1, b_buf, xg, acc, h_t, h_r, part, tx, rx, own,
-    sc_own, sc_all, o_buf, q1, q2, home, gw,
-    w_sem, ow_sem, a1_send, a1_recv, a2_send, a2_recv, ag_send, ag_recv, rs_send, rs_recv,
+    tok_h, gout_h, rt_h, pt_h, wg_h, wu_h, wd_h,
+    mixed, gtok, gprob, gw_g, gw_u, gw_d,
+    tok, gout, rt, pt, wg, wu, wd, disp, disp_t, s_buf, r1, b_buf, xg, acc, h_t, h_r, part, tx, rx, own,
+    sc_own, sc_all, o_buf, q1, q2, home,
+    w_sem, a1_send, a1_recv, a2_send, a2_recv, ag_send, ag_recv, rs_send, rs_recv,
     sc_send, sc_recv, b1_send, b1_recv, b2_send, b2_recv,
 ):
     e = lax.axis_index("expert")
@@ -34,7 +34,6 @@
     x_me = e // (2 * ny)
     y_me = (e // 2) % ny
     xc_me = x_me * 2 + e % 2
-    half = nz // 2
     rows = ny * nxc * 2
     nt = tok.shape[0]
     topk = rt.shape[0]
@@ -50,11 +49,10 @@
     def z_at(d):
         return lax.rem(m + d + 2 * nz, nz)
 
-    right, left = z_at(1), z_at(-1)
-
     loads = [
         pltpu.make_async_copy(src, dst, w_sem.at[i])
-        for i, (src, dst) in enumerate(((wg_h, wg), (wu_h, wu), (wd_h, wd)))
+        for i, (src, dst) in enumerate(
+            ((rt_h, rt), (pt_h, pt), (tok_h, tok), (gout_h, gout), (wg_h, wg), (wu_h, wu), (wd_h, wd)))
     ]
     for c in loads:
         c.start()
@@ -67,6 +65,8 @@
     for d in range(1, nz):
         pl.semaphore_signal(barrier, inc=1, device_id={"mp": z_at(d)}, device_id_type=MESH)
 
+    for c in loads[:4]:
+        c.wait()
     r = lax.broadcasted_iota(jnp.int32, (rows, nt), 0)
     sy = nxc * 2
     y_r = r // sy
@@ -147,18 +147,24 @@
 
     a2 = send_xc(b_buf, xg.at[m], a2_send, a2_recv)
     pending += a2
-    for c in loads:
+    for c in loads[4:]:
         c.wait()
     for c in a2:
         c.wait_recv()
 
-    def hop(way, a, s):
-        to, sign = ((right, -1), (left, 1))[way]
-        blk = z_at(sign * (s - 1))
+    def give(a, o, to):
+        blk = z_at(-o)
         return pltpu.make_async_remote_copy(
             src_ref=xg.at[blk, a], dst_ref=xg.at[blk, a],
-            send_sem=ag_send.at[way, a, s], recv_sem=ag_recv.at[way, a, s],
-            device_id={"mp": to}, device_id_type=MESH)
+            send_sem=ag_send.at[a, to % nz], recv_sem=ag_recv.at[a, to % nz],
+            device_id={"mp": z_at(to - o)}, device_id_type=MESH)
+
+    def got(a, o):
+        blk = z_at(-o)
+        pltpu.make_async_remote_copy(
+            src_ref=xg.at[blk, a], dst_ref=xg.at[blk, a],
+            send_sem=ag_send.at[a, o % nz], recv_sem=ag_recv.at[a, o % nz],
+            device_id={"mp": z_at(1)}, device_id_type=MESH).wait_recv()
 
     def cols(blk):
         return pl.ds(pl.multiple_of(blk * 128, 128), 128)
@@ -171,35 +177,55 @@
         else:
             acc[2] += dot_nt(wd[:, cols(blk)], v)
 
-    def last(way, a):
-        return half if way == a else half - 1
-
-    for a in range(2):
-        for way in range(2):
-            hop(way, a, 1).start()
-    for a in range(2):
-        use(m, a)
-
-    def ag_step(s, full):
-        for a in range(2):
-            for way in range(2):
-                hop(way, a, s).wait_recv()
-                if full or s < last(way, a):
-                    hop(way, a, s + 1).start()
-        for a in range(2):
-            for way in range(2):
-                use(z_at((-1, 1)[way] * s), a)
-
-    def ag_body(s, carry):
-        ag_step(s, True)
-        return carry
-
-    lax.fori_loop(1, half - 1, ag_body, 0)
-    ag_step(half - 1, False)
-    for a in range(2):
-        hop(a, a, half).wait_recv()
-    for a in range(2):
-        use(z_at(half), a)
+    def far(a):
+        return 8 if a == 0 else -8
+
+    for to in (3, -3, 1, -1):
+        for a in range(2):
+            give(a, 0, to).start()
+
+    def use_at(o):
+        for a in range(2):
+            use(z_at(-o), a)
+
+    use_at(0)
+    for a in range(2):
+        for g in (1, -1):
+            got(a, 3 * g)
+            for to in (6, 4, 2):
+                give(a, 3 * g, to * g).start()
+    for o in (3, -3):
+        use_at(o)
+    for o in (1, -1):
+        for a in range(2):
+            got(a, o)
+        use_at(o)
+    for a in range(2):
+        for g in (1, -1):
+            got(a, 6 * g)
+            if far(a) * g > 0:
+                give(a, 6 * g, 8 * g).start()
+            for to in (7, 5):
+                give(a, 6 * g, to * g).start()
+
+    def use_many(base, n):
+        def body(i, carry):
+            o = (1 - 2 * (i % 2)) * (base + 2 * (i // 2))
+            for a in range(2):
+                got(a, o)
+            for a in range(2):
+                use(z_at(-o), a)
+            return carry
+
+        lax.fori_loop(0, n, body, 0)
+
+    use_many(2, 4)
+    for o in (6, -6):
+        use_at(o)
+    use_many(5, 4)
+    for a in range(2):
+        got(a, far(a))
+        use(z_at(-far(a)), a)
 
     gate, up, back = acc[0], acc[1], acc[2]
     sig = jax.nn.sigmoid(gate)
@@ -220,63 +246,77 @@
         h_r[i] = jnp.transpose(v).astype(BF)
         h_t[i] = v.astype(BF)
 
-    def blk_at(way, a, s):
-        n = last(way, a)
-        return z_at(n + 1 - s) if way == 0 else z_at(s - n - 1)
-
     def partial(a, blk):
         if a == 0:
             return dot(h_r[0], wd[:, cols(blk)])
         return dot(h_r[1], wg[:, cols(blk)]) + dot(h_r[2], wu[:, cols(blk)])
 
-    def turn(way, a, s):
+    def turn(a, o, to):
         return pltpu.make_async_remote_copy(
-            src_ref=tx.at[way, a, s], dst_ref=rx.at[way, a, s],
-            send_sem=rs_send.at[way, a, s], recv_sem=rs_recv.at[way, a, s],
-            device_id={"mp": (right, left)[way]}, device_id_type=MESH)
+            src_ref=tx.at[a, o % nz], dst_ref=rx.at[a, o % nz],
+            send_sem=rs_send.at[a, o % nz], recv_sem=rs_recv.at[a, o % nz],
+            device_id={"mp": z_at(to - o)}, device_id_type=MESH)
+
+    def came(a, o):
+        turn(a, o, o + 1).wait_recv()
+        return rx[a, o % nz].astype(F32)
 
     def weights_of(blk):
         x_v, g_v = xg[blk, 0], xg[blk, 1]
-        gw[0, :, cols(blk)] = dot(h_t[1], x_v).astype(BF)
-        gw[1, :, cols(blk)] = dot(h_t[2], x_v).astype(BF)
-        gw[2, :, cols(blk)] = dot(h_t[0], g_v).astype(BF)
-
-    for a in range(2):
-        for way in range(2):
-            tx[way, a, 1] = partial(a, blk_at(way, a, 1)).astype(BF)
-            turn(way, a, 1).start()
-    for a in range(2):
-        for way in range(2):
-            part[way, a] = partial(a, blk_at(way, a, 2))
-    weights_of(0)
-    weights_of(1)
-
-    def rs_step(s, full):
-        for a in range(2):
-            for way in range(2):
-                if full or s <= last(way, a):
-                    turn(way, a, s - 1).wait_recv()
-                    tx[way, a, s] = (part[way, a] + rx[way, a, s - 1].astype(F32)).astype(BF)
-                    turn(way, a, s).start()
-        for a in range(2):
-            for way in range(2):
-                if full or s + 1 <= last(way, a):
-                    part[way, a] = partial(a, blk_at(way, a, s + 1))
-        weights_of(2 * s - 2)
-        weights_of(2 * s - 1)
-
-    def rs_body(s, carry):
-        rs_step(s, True)
-        return carry
-
-    lax.fori_loop(2, half - 1, rs_body, 0)
-    for s in range(max(2, half - 1), half + 1):
-        rs_step(s, False)
-    out_w = [pltpu.make_async_copy(gw.at[i], ref, ow_sem.at[i]) for i, ref in enumerate((ogg, ogu, ogd))]
-    for c in out_w:
-        c.start()
+        gw_g[:, cols(blk)] = dot(h_t[1], x_v).astype(BF)
+        gw_u[:, cols(blk)] = dot(h_t[2], x_v).astype(BF)
+        gw_d[:, cols(blk)] = dot(h_t[0], g_v).astype(BF)
+
+    def weights_from(first, last):
+        def body(i, carry):
+            weights_of(i)
+            return carry
+
+        lax.fori_loop(first, last, body, 0)
+
+    def leaf(a, o, to):
+        tx[a, o % nz] = partial(a, z_at(-o)).astype(BF)
+        turn(a, o, to).start()
+
+    def leaves(centre):
+        def body(i, carry):
+            g = 1 - 2 * (i % 2)
+            o = g * (centre - 1 + 2 * (i // 2))
+            for a in range(2):
+                leaf(a, o, g * centre)
+            return carry
+
+        lax.fori_loop(0, 4, body, 0)
+
+    for a in range(2):
+        leaf(a, far(a), far(a) * 6 // 8)
+    leaves(6)
+    leaves(3)
+    for g in range(2):
+        for a in range(2):
+            part[g, a] = partial(a, z_at((-6, 6)[g]))
+    for a in range(2):
+        for g in range(2):
+            sign = (1, -1)[g]
+            total = part[g, a] + came(a, 5 * sign) + came(a, 7 * sign)
+            if far(a) * sign > 0:
+                total = total + came(a, 8 * sign)
+            tx[a, 6 * sign % nz] = total.astype(BF)
+            turn(a, 6 * sign, 3 * sign).start()
+    for g in range(2):
+        for a in range(2):
+            leaf(a, (1, -1)[g], 0)
+            part[g, a] = partial(a, z_at((-3, 3)[g]))
+    weights_from(0, 6)
+    for a in range(2):
+        for g in range(2):
+            sign = (1, -1)[g]
+            total = part[g, a] + came(a, 2 * sign) + came(a, 4 * sign) + came(a, 6 * sign)
+            tx[a, 3 * sign % nz] = total.astype(BF)
+            turn(a, 3 * sign, 0).start()
     for a in range(2):
         own[a] = partial(a, m)
+    weights_from(6, 16)
 
     sc_all[m] = sc_own[...]
     for c in scores:
@@ -289,10 +329,8 @@
 
     for a in range(2):
         total = own[a]
-        for way in (1 - a, a):
-            n = last(way, a)
-            turn(way, a, n).wait_recv()
-            total = total + rx[way, a, n].astype(F32)
+        for o in (1, -1, 3, -3):
+            total = total + came(a, o)
         o_buf[a] = total.astype(BF)
 
     b1 = send_xc(o_buf, q1, b1_send, b1_recv)
@@ -306,14 +344,10 @@
 
     for c in pending:
         c.wait_send()
-    for s in range(1, half + 1):
-        for a in range(2):
-            for way in range(2):
-                if s <= last(way, a):
-                    hop(way, a, s).wait_send()
-                    turn(way, a, s).wait_send()
-    for c in out_w:
-        c.wait()
+    for o in range(1, nz):
+        for a in range(2):
+            give(a, 0, o).wait_send()
+            turn(a, o, 0).wait_send()
     for c in b2:
         c.wait_recv()
 
@@ -326,53 +360,71 @@
         gprob[k : k + 1, :] = picked / pt[k : k + 1, :]
 
 
+def write_out(*refs):
+    n = len(refs) // 2
+    sems = refs[-1]
+    copies = [pltpu.make_async_copy(refs[i], refs[n + i], sems.at[i]) for i in range(n)]
+    for c in copies:
+        c.start()
+    for c in copies:
+        c.wait()
+
+
 def local(ny, nxc, nz, tokens, routes, probs, w_gate, w_up, w_down, grad_out):
     nt, width = tokens.shape
     topk = routes.shape[1]
     d, f = w_gate.shape[1:]
     rows = ny * nxc * 2
-    half = nz // 2
     vmem = pl.BlockSpec(memory_space=pltpu.VMEM)
     hbm = pl.BlockSpec(memory_space=pl.ANY)
     dma = pltpu.SemaphoreType.DMA
     V = pltpu.VMEM
+    shapes = (
+        jax.ShapeDtypeStruct((nt, width), BF),
+        jax.ShapeDtypeStruct((nt, width), BF),
+        jax.ShapeDtypeStruct((topk, nt), F32),
+        jax.ShapeDtypeStruct((f, d), BF),
+        jax.ShapeDtypeStruct((f, d), BF),
+        jax.ShapeDtypeStruct((f, d), BF),
+    )
     outs = pl.pallas_call(
         functools.partial(kernel, ny, nxc, nz),
-        out_shape=(
-            jax.ShapeDtypeStruct((nt, width), BF),
-            jax.ShapeDtypeStruct((nt, width), BF),
-            jax.ShapeDtypeStruct((topk, nt), F32),
-            jax.ShapeDtypeStruct((f, d), BF),
-            jax.ShapeDtypeStruct((f, d), BF),
-            jax.ShapeDtypeStruct((f, d), BF),
-        ),
-        in_specs=[vmem] * 4 + [hbm] * 3,
-        out_specs=(vmem, vmem, vmem, hbm, hbm, hbm),
+        out_shape=tuple(pltpu.VMEM(t.shape, t.dtype) for t in shapes),
+        in_specs=[hbm] * 7,
+        out_specs=(vmem,) * 6,
         scratch_shapes=[
+            V((nt, width), BF), V((nt, width), BF), V((topk, nt), jnp.int32), V((topk, nt), F32),
             V((f, d), BF), V((f, d), BF), V((f, d), BF),
             V((rows, nt), F32), V((3, nt, rows), BF),
             V((2, rows, width), BF), V((2, rows, width), BF), V((2, rows, width), BF),
             V((nz, 2, rows, width), BF),
             V((3, f, rows), F32), V((3, f, rows), BF), V((3, rows, f), BF),
             V((2, 2, rows, width), F32),
-            V((2, 2, half + 1, rows, width), BF), V((2, 2, half + 1, rows, width), BF),
+            V((2, nz, rows, width), BF), V((2, nz, rows, width), BF),
             V((2, rows, width), F32),
             V((8, rows), F32), V((nz, 8, rows), F32),
             V((3, rows, width), BF), V((3, rows, width), BF), V((3, rows, width), BF), V((3, rows, width), BF),
-            V((3, f, d), BF),
-            dma((3,)), dma((3,)),
+            dma((7,)),
             dma((ny,)), dma((ny,)), dma((nxc,)), dma((nxc,)),
-            dma((2, 2, half + 1)), dma((2, 2, half + 1)), dma((2, 2, half + 1)), dma((2, 2, half + 1)),
+            dma((2, nz)), dma((2, nz)), dma((2, nz)), dma((2, nz)),
             dma((nz,)), dma((nz,)),
             dma((nxc,)), dma((nxc,)), dma((ny,)), dma((ny,)),
         ],
         compiler_params=pltpu.CompilerParams(
-            collective_id=0, has_side_effects=True, vmem_limit_bytes=24 * 1024 * 1024
+            collective_id=0, has_side_effects=True, vmem_limit_bytes=65700000
         ),
     )(
         tokens, grad_out, routes.T, probs.T,
         jnp.swapaxes(w_gate, 1, 2).reshape(f, d), jnp.swapaxes(w_up, 1, 2).reshape(f, d), w_down.reshape(f, d),
     )
+    outs = pl.pallas_call(
+        write_out,
+        out_shape=shapes,
+        in_specs=[hbm] * 6,
+        out_specs=(pl.BlockSpec(memory_space=pltpu.HBM),) * 6,
+        scratch_shapes=[dma((6,))],
+        compiler_params=pltpu.CompilerParams(vmem_limit_bytes=1024 * 1024),
+    )(*outs)
     mixed, gtok, gprob, gg, gu, gd = outs
     return (
         mixed, gtok, gprob.T,

time: 108 us -> 86.7 us (0.80)
  Pallas kernels: 98.2 us -> 85.9 us
  local copies, waits for them, and re-layouts: 8.99 us -> 0 us
    pallas_call x1 -> x2, Pallas kernels: 98.2 us -> 85.9 us  [the longest x1 84.8 us: local(): pl.pallas_call(functools.partial(kernel, ny, nxc, nz), out_shape=tuple((p...]
    unnamed x20 -> x0, local copies, waits for them, and re-layouts: 8.99 us -> none
where the time goes in v2:
time: 86.7 us; the launch traced here: 86.5 us
  Pallas kernels  85.9 us (99%)
    pallas_call x1, Pallas kernels, local(): pl.pallas_call(functools.partial(kernel, ny, nxc, nz), out_shape=tuple((p...  84.8 us

profile of v2, /device:TPU:1, one launch (start us, length us, event | category | flops | bytes accessed | tf_op | source)
XLA Modules:
  0.0 86.5 jit_solution(6950792123841555661)
XLA Ops:
  0.6 84.8 %shard_map.118 = (bf16[16,128]{1,0:T(8,128)(2,1)S(1)}, bf16[16,128]{1,0:T(8,128)(2,1)S(1)}, f32[6,16]{1,0:T(8,128)S(1)}, bf16[88,2048]{1,0:T(8,128)(2,1)S(1)}, b...) custom-call(bf16[16,128]{1,0:T(8,128)(2,1)} %tok_h.1, bf16[16,128]{1,0:T(8,128)(2,1)} %gout_h.1, ...), custom_call_target="tpu_custom_call" | custom-call | tf_op jit(solution)/shard_map/pallas_call | solution.py:390
  85.5 1.0 %shard_map.119 = (bf16[16,128]{1,0:T(8,128)(2,1)}, bf16[16,128]{1,0:T(8,128)(2,1)}, f32[6,16]{1,0:T(8,128)}, bf16[88,2048]{1,0:T(8,128)(2,1)}, bf16[88,2048]{1,0:T(8,128)(2,1)}, /*index=5*/bf16[88,2048]{1,0:T(8,128)(2,1)}) custom-call(bf16[16,128]{1,0:T(8,128)(2,1)S(1)} %get-tuple-element.18.refs_0_, bf16[16,128]{1,0:T(8,128)(2,1)S(1)} %get-tuple-element.19.refs_1_, ...), custom_call_target="tpu_custom_call" | custom-call | tf_op jit(solution)/shard_map/pallas_call | solution.py:420

commit v3 on v2

v3 whole, which is shorter than its diff:
```python
import functools

import jax
import jax.numpy as jnp
from jax import lax
from jax.experimental import pallas as pl
from jax.experimental.pallas import tpu as pltpu
from jax.sharding import PartitionSpec as P

MESH = pl.DeviceIdType.MESH
BF = jnp.bfloat16
F32 = jnp.float32


def dot(a, b):
    return jnp.dot(a, b, preferred_element_type=F32)


def dot_nt(a, b):
    return lax.dot_general(a, b, (((1,), (1,)), ((), ())), preferred_element_type=F32)


def kernel(
    ne, nz,
    tok_h, gout_h, rt_h, pt_h, wg_h, wu_h, wd_h,
    mixed, gtok, gprob, gw_g, gw_u, gw_d,
    tok, gout, rt, pt, wg, wu, wd, disp, disp_t, s_buf, r_buf, xg, acc, h_t, h_r, part, tx, rx, own,
    sc_all, o_buf, o_home, b_buf, b_home,
    w_sem, a2a_send, a2a_recv, ag_send, ag_recv, rs_send, rs_recv, sc_send, sc_recv,
):
    e = lax.axis_index("expert")
    m = lax.axis_index("mp")
    rows = 2 * ne
    nt = tok.shape[0]
    topk = rt.shape[0]

    def z_at(d):
        return lax.rem(m + d + 2 * nz, nz)

    loads = [
        pltpu.make_async_copy(src, dst, w_sem.at[i])
        for i, (src, dst) in enumerate(
            ((rt_h, rt), (pt_h, pt), (tok_h, tok), (gout_h, gout), (wg_h, wg), (wu_h, wu), (wd_h, wd)))
    ]
    for c in loads:
        c.start()

    barrier = pltpu.get_barrier_semaphore()
    def greet(d, carry):
        pl.semaphore_signal(barrier, inc=1, device_id={"expert": lax.rem(e + d, ne)}, device_id_type=MESH)
        return carry

    lax.fori_loop(1, ne, greet, 0)
    near = (1, -1, 2, -2, 3, -3)
    for d in near:
        pl.semaphore_signal(barrier, inc=1, device_id={"mp": z_at(d)}, device_id_type=MESH)

    for c in loads[:4]:
        c.wait()
    r = lax.broadcasted_iota(jnp.int32, (rows, nt), 0)
    slot_r = r // ne
    e_r = r % ne
    chosen = jnp.zeros((rows, nt), F32)
    weight = jnp.zeros((rows, nt), F32)
    for k in range(topk):
        hit = rt[k : k + 1, :] == e_r
        chosen = jnp.where(hit, 1.0, chosen)
        weight = jnp.where(hit, pt[k : k + 1, :], weight)
    t0 = lax.broadcasted_iota(jnp.int32, (nt, nt), 0)
    t1 = lax.broadcasted_iota(jnp.int32, (nt, nt), 1)
    earlier = jnp.where(t0 < t1, 1.0, 0.0).astype(BF)
    before = dot(chosen.astype(BF), earlier)
    d_f = jnp.where(before == slot_r.astype(F32), chosen, 0.0)
    d_w = d_f * weight
    disp[...] = d_f
    d_b = d_f.astype(BF)
    w_row = jnp.sum(d_w, axis=1, keepdims=True)
    v_in = dot(d_b, tok[...])
    v_grad = dot(d_b, gout[...]) * w_row

    def put(ref, i, v):
        ref[:, 0, 128 * i : 128 * (i + 1)] = v[:ne]
        ref[:, 0, 128 * (i + 1) : 128 * (i + 2)] = v[ne:]

    def take(ref, i):
        return jnp.concatenate(
            [ref[:, 0, 128 * i : 128 * (i + 1)], ref[:, 0, 128 * (i + 1) : 128 * (i + 2)]], axis=0).astype(BF)

    put(s_buf, 0, v_in)
    put(s_buf, 2, v_grad)

    pl.semaphore_wait(barrier, (ne - 1) + len(near))

    def to_all(i, src, dst):
        def body(d, carry):
            peer = lax.rem(e + d, ne)
            pltpu.make_async_remote_copy(
                src_ref=src.at[peer], dst_ref=dst.at[e], send_sem=a2a_send.at[i], recv_sem=a2a_recv.at[i],
                device_id={"expert": peer}, device_id_type=MESH).start()
            return carry

        lax.fori_loop(1, ne, body, 0)
        dst[e] = src[e]

    def all_of(i, src, dst):
        return pltpu.make_async_remote_copy(
            src_ref=src.at[pl.ds(0, ne - 1)], dst_ref=dst.at[pl.ds(0, ne - 1)],
            send_sem=a2a_send.at[i], recv_sem=a2a_recv.at[i],
            device_id={"expert": lax.rem(e + 1, ne)}, device_id_type=MESH)

    to_all(0, s_buf, r_buf)

    t_f = jnp.transpose(d_f)
    t_w = jnp.transpose(d_w)
    t_hi = t_w.astype(BF)
    disp_t[0] = t_hi
    disp_t[1] = (t_w - t_hi.astype(F32)).astype(BF)
    disp_t[2] = t_f.astype(BF)
    for a in range(3):
        acc[a] = jnp.zeros(acc.shape[1:], F32)

    for c in loads[4:]:
        c.wait()
    all_of(0, s_buf, r_buf).wait_recv()
    for a in range(2):
        xg[m, a] = take(r_buf, 2 * a)

    def give(a, o, to):
        blk = z_at(-o)
        return pltpu.make_async_remote_copy(
            src_ref=xg.at[blk, a], dst_ref=xg.at[blk, a],
            send_sem=ag_send.at[a, to % nz], recv_sem=ag_recv.at[a, to % nz],
            device_id={"mp": z_at(to - o)}, device_id_type=MESH)

    def got(a, o):
        blk = z_at(-o)
        pltpu.make_async_remote_copy(
            src_ref=xg.at[blk, a], dst_ref=xg.at[blk, a],
            send_sem=ag_send.at[a, o % nz], recv_sem=ag_recv.at[a, o % nz],
            device_id={"mp": z_at(1)}, device_id_type=MESH).wait_recv()

    def cols(blk):
        return pl.ds(pl.multiple_of(blk * 128, 128), 128)

    def use(blk, a):
        v = xg[blk, a]
        if a == 0:
            acc[0] += dot_nt(wg[:, cols(blk)], v)
            acc[1] += dot_nt(wu[:, cols(blk)], v)
        else:
            acc[2] += dot_nt(wd[:, cols(blk)], v)

    def far(a):
        return 8 if a == 0 else -8

    def pass3(a):
        for g in (1, -1):
            got(a, 3 * g)
            for to in (6, 4, 2):
                give(a, 3 * g, to * g).start()

    def pass6(a):
        for g in (1, -1):
            got(a, 6 * g)
            if far(a) * g > 0:
                give(a, 6 * g, 8 * g).start()
            for to in (7, 5):
                give(a, 6 * g, to * g).start()

    def use_at(a, *offsets):
        for o in offsets:
            use(z_at(-o), a)

    def use_many(a, base, n):
        def body(i, carry):
            o = (1 - 2 * (i % 2)) * (base + 2 * (i // 2))
            got(a, o)
            use(z_at(-o), a)
            return carry

        lax.fori_loop(0, n, body, 0)

    for a in range(2):
        for to in (3, -3, 1, -1):
            give(a, 0, to).start()
    use_at(0, 0)
    pass3(0)
    use_at(0, 3, -3)
    pass3(1)
    use_many(0, 1, 2)
    use_at(1, 0, 3, -3)
    pass6(0)
    use_many(0, 2, 4)
    use_at(0, 6, -6)
    pass6(1)
    use_many(0, 5, 4)
    got(0, far(0))
    use_at(0, far(0))

    def keep(i, v):
        h_r[i] = jnp.transpose(v).astype(BF)
        h_t[i] = v.astype(BF)

    gate, up = acc[0], acc[1]
    keep(0, gate * jax.nn.sigmoid(gate) * up)

    def partial(a, blk):
        if a == 0:
            return dot(h_r[0], wd[:, cols(blk)])
        return dot(h_r[1], wg[:, cols(blk)]) + dot(h_r[2], wu[:, cols(blk)])

    def turn(a, o, to):
        return pltpu.make_async_remote_copy(
            src_ref=tx.at[a, o % nz], dst_ref=rx.at[a, o % nz],
            send_sem=rs_send.at[a, o % nz], recv_sem=rs_recv.at[a, o % nz],
            device_id={"mp": z_at(to - o)}, device_id_type=MESH)

    def came(a, o):
        turn(a, o, o + 1).wait_recv()
        return rx[a, o % nz].astype(F32)

    def weights_of(blk):
        x_v, g_v = xg[blk, 0], xg[blk, 1]
        gw_g[:, cols(blk)] = dot(h_t[1], x_v).astype(BF)
        gw_u[:, cols(blk)] = dot(h_t[2], x_v).astype(BF)
        gw_d[:, cols(blk)] = dot(h_t[0], g_v).astype(BF)

    def weights_from(first, last):
        def body(i, carry):
            weights_of(i)
            return carry

        lax.fori_loop(first, last, body, 0)

    def leaf(a, o, to):
        tx[a, o % nz] = partial(a, z_at(-o)).astype(BF)
        turn(a, o, to).start()

    def leaves(a):
        leaf(a, far(a), far(a) * 6 // 8)

        def body(i, carry):
            g = 1 - 2 * (i % 2)
            centre = 6 - 3 * (i // 4)
            o = centre - 1 + 2 * ((i // 2) % 2)
            leaf(a, g * o, g * centre)
            return carry

        lax.fori_loop(0, 8, body, 0)

    def leaves1(a):
        for g in (1, -1):
            leaf(a, g, 0)

    def part_of(a, o):
        for g in range(2):
            part[g, a] = partial(a, z_at((-o, o)[g]))

    def mid(a, o, to, kids):
        for g in range(2):
            sign = (1, -1)[g]
            total = part[g, a]
            for k in kids:
                if k < 8 or far(a) * sign > 0:
                    total = total + came(a, k * sign)
            tx[a, o * sign % nz] = total.astype(BF)
            turn(a, o * sign, to * sign).start()

    def final(a):
        total = own[a]
        for o in (1, -1, 3, -3):
            total = total + came(a, o)
        put((o_buf, b_buf)[a], 0, total)

    def give_sc(o, to):
        return pltpu.make_async_remote_copy(
            src_ref=sc_all.at[z_at(-o)], dst_ref=sc_all.at[z_at(-o)],
            send_sem=sc_send.at[to % nz], recv_sem=sc_recv.at[to % nz],
            device_id={"mp": z_at(to - o)}, device_id_type=MESH)

    def got_sc(o):
        pltpu.make_async_remote_copy(
            src_ref=sc_all.at[z_at(-o)], dst_ref=sc_all.at[z_at(-o)],
            send_sem=sc_send.at[o % nz], recv_sem=sc_recv.at[o % nz],
            device_id={"mp": z_at(1)}, device_id_type=MESH).wait_recv()

    leaves(0)
    leaves1(0)
    part_of(0, 6)

    use_many(1, 1, 2)
    use_many(1, 2, 4)
    use_at(1, 6, -6)
    use_many(1, 5, 4)
    got(1, far(1))
    use_at(1, far(1))
    gate, up, back = acc[0], acc[1], acc[2]
    sig = jax.nn.sigmoid(gate)
    silu = gate * sig
    keep(1, back * up * sig * (1.0 + gate * (1.0 - sig)))
    keep(2, back * silu)
    mid(0, 6, 3, (5, 7, 8))
    sc_all[m] = jnp.broadcast_to(jnp.sum(silu * up * back, axis=0, keepdims=True), sc_all.shape[1:])
    leaves(1)
    for to in (3, -3, 1, -1):
        give_sc(0, to).start()
    part_of(0, 3)
    part_of(1, 6)
    mid(0, 3, 0, (2, 4, 6))
    mid(1, 6, 3, (5, 7, 8))
    leaves1(1)
    for g in (1, -1):
        got_sc(3 * g)
        for to in (6, 4, 2):
            give_sc(3 * g, to * g).start()
    part_of(1, 3)
    for a in range(2):
        own[a] = partial(a, m)
    weights_from(0, 5)

    final(0)
    to_all(1, o_buf, o_home)
    mid(1, 3, 0, (2, 4, 6))
    for g in (1, -1):
        got_sc(6 * g)
        for to in (7, 5):
            give_sc(6 * g, to * g).start()
    give_sc(6, 8).start()
    weights_from(5, 16)

    for o in (1, -1, 2, -2, 4, -4, 5, -5, 7, -7, 8):
        got_sc(o)
    sc = jnp.broadcast_to(jnp.sum(sc_all[...], axis=0)[0:1, :], (ne, rows))
    row = lax.broadcasted_iota(jnp.int32, (ne, rows), 0)
    col = lax.broadcasted_iota(jnp.int32, (ne, rows), 1)
    sc_col = [jnp.sum(jnp.where(col == row + ne * i, sc, 0.0), axis=1, keepdims=True) for i in range(2)]
    lane = lax.broadcasted_iota(jnp.int32, (ne, 128), 1)
    b_buf[:, 0, 256:384] = jnp.where(lane == 0, sc_col[0], jnp.where(lane == 1, sc_col[1], 0.0))

    final(1)
    to_all(2, b_buf, b_home)

    all_of(1, o_buf, o_home).wait_recv()
    out = take(o_home, 0)
    mixed[...] = (dot(disp_t[0], out) + dot(disp_t[1], out)).astype(BF)

    for i, refs in enumerate(((s_buf, r_buf), (o_buf, o_home), (b_buf, b_home))):
        all_of(i, *refs).wait_send()
    for o in range(1, nz):
        for a in range(2):
            give(a, 0, o).wait_send()
            turn(a, o, 0).wait_send()
        give_sc(0, o).wait_send()
    all_of(2, b_buf, b_home).wait_recv()

    gtok[...] = dot(disp_t[2], take(b_home, 0)).astype(BF)
    score = b_home[:, 0, 256:384]
    score = disp[...] * jnp.concatenate([score[:, 0:1], score[:, 1:2]], axis=0)
    for k in range(topk):
        picked = jnp.sum(jnp.where(rt[k : k + 1, :] == e_r, score, 0.0), axis=0, keepdims=True)
        gprob[k : k + 1, :] = picked / pt[k : k + 1, :]


def write_out(*refs):
    n = len(refs) // 2
    sems = refs[-1]
    copies = [pltpu.make_async_copy(refs[i], refs[n + i], sems.at[i]) for i in range(n)]
    for c in copies:
        c.start()
    for c in copies:
        c.wait()


def local(ne, nz, tokens, routes, probs, w_gate, w_up, w_down, grad_out):
    nt, width = tokens.shape
    topk = routes.shape[1]
    d, f = w_gate.shape[1:]
    rows = ne * 2
    vmem = pl.BlockSpec(memory_space=pltpu.VMEM)
    hbm = pl.BlockSpec(memory_space=pl.ANY)
    dma = pltpu.SemaphoreType.DMA
    V = pltpu.VMEM
    shapes = (
        jax.ShapeDtypeStruct((nt, width), BF),
        jax.ShapeDtypeStruct((nt, width), BF),
        jax.ShapeDtypeStruct((topk, nt), F32),
        jax.ShapeDtypeStruct((f, d), BF),
        jax.ShapeDtypeStruct((f, d), BF),
        jax.ShapeDtypeStruct((f, d), BF),
    )
    outs = pl.pallas_call(
        functools.partial(kernel, ne, nz),
        out_shape=tuple(pltpu.VMEM(t.shape, t.dtype) for t in shapes),
        in_specs=[hbm] * 7,
        out_specs=(vmem,) * 6,
        scratch_shapes=[
            V((nt, width), BF), V((nt, width), BF), V((topk, nt), jnp.int32), V((topk, nt), F32),
            V((f, d), BF), V((f, d), BF), V((f, d), BF),
            V((rows, nt), F32), V((3, nt, rows), BF),
            V((ne, 1, 512), F32), V((ne, 1, 512), F32),
            V((nz, 2, rows, width), BF),
            V((3, f, rows), F32), V((3, f, rows), BF), V((3, rows, f), BF),
            V((2, 2, rows, width), F32),
            V((2, nz, rows, width), BF), V((2, nz, rows, width), BF),
            V((2, rows, width), F32),
            V((nz, 8, rows), F32),
            V((ne, 1, 256), F32), V((ne, 1, 256), F32), V((ne, 1, 384), F32), V((ne, 1, 384), F32),
            dma((7,)), dma((3,)), dma((3,)),
            dma((2, nz)), dma((2, nz)), dma((2, nz)), dma((2, nz)),
            dma((nz,)), dma((nz,)),
        ],
        compiler_params=pltpu.CompilerParams(
            collective_id=0, has_side_effects=True, vmem_limit_bytes=65700000
        ),
    )(
        tokens, grad_out, routes.T, probs.T,
        jnp.swapaxes(w_gate, 1, 2).reshape(f, d), jnp.swapaxes(w_up, 1, 2).reshape(f, d), w_down.reshape(f, d),
    )
    outs = pl.pallas_call(
        write_out,
        out_shape=shapes,
        in_specs=[hbm] * 6,
        out_specs=(pl.BlockSpec(memory_space=pltpu.HBM),) * 6,
        scratch_shapes=[dma((6,))],
        compiler_params=pltpu.CompilerParams(vmem_limit_bytes=1024 * 1024),
    )(*outs)
    mixed, gtok, gprob, gg, gu, gd = outs
    return (
        mixed, gtok, gprob.T,
        jnp.swapaxes(gg.reshape(1, f, d), 1, 2), jnp.swapaxes(gu.reshape(1, f, d), 1, 2), gd.reshape(1, f, d),
    )


def solution(mesh):
    ne, nz = mesh.shape["expert"], mesh.shape["mp"]
    placed = (
        P("expert", "mp"),
        P("expert", None),
        P("expert", None),
        P("expert", None, "mp"),
        P("expert", None, "mp"),
        P("expert", "mp", None),
        P("expert", "mp"),
    )
    return jax.shard_map(
        functools.partial(local, ne, nz),
        mesh=mesh,
        in_specs=placed,
        out_specs=(
            P("expert", "mp"),
            P("expert", "mp"),
            P("expert", None),
            P("expert", None, "mp"),
            P("expert", None, "mp"),
            P("expert", "mp", None),
        ),
        check_vma=False,
    )
```

time: 86.7 us -> 85.5 us (0.986)
  Pallas kernels: 85.9 us -> 84.8 us
    pallas_call x1, Pallas kernels: 84.8 us -> 83.7 us  [local(): pl.pallas_call(functools.partial(kernel, ne, nz), out_shape=tuple((pltpu....]
where the time goes in v3:
time: 85.5 us; the launch traced here: 85.4 us
  Pallas kernels  84.8 us (99%)
    pallas_call x1, Pallas kernels, local(): pl.pallas_call(functools.partial(kernel, ne, nz), out_shape=tuple((pltpu....  83.7 us

profile of v3, /device:TPU:1, one launch (start us, length us, event | category | flops | bytes accessed | tf_op | source)
XLA Modules:
  0.0 85.4 jit_solution(12108931667937405736)
XLA Ops:
  0.6 83.7 %shard_map.118 = (bf16[16,128]{1,0:T(8,128)(2,1)S(1)}, bf16[16,128]{1,0:T(8,128)(2,1)S(1)}, f32[6,16]{1,0:T(8,128)S(1)}, bf16[88,2048]{1,0:T(8,128)(2,1)S(1)}, b...) custom-call(bf16[16,128]{1,0:T(8,128)(2,1)} %tok_h.1, bf16[16,128]{1,0:T(8,128)(2,1)} %gout_h.1, ...), custom_call_target="tpu_custom_call" | custom-call | tf_op jit(solution)/shard_map/pallas_call | solution.py:391
  84.4 1.0 %shard_map.119 = (bf16[16,128]{1,0:T(8,128)(2,1)}, bf16[16,128]{1,0:T(8,128)(2,1)}, f32[6,16]{1,0:T(8,128)}, bf16[88,2048]{1,0:T(8,128)(2,1)}, bf16[88,2048]{1,0:T(8,128)(2,1)}, /*index=5*/bf16[88,2048]{1,0:T(8,128)(2,1)}) custom-call(bf16[16,128]{1,0:T(8,128)(2,1)S(1)} %get-tuple-element.18.refs_0_, bf16[16,128]{1,0:T(8,128)(2,1)S(1)} %get-tuple-element.19.refs_1_, ...), custom_call_target="tpu_custom_call" | custom-call | tf_op jit(solution)/shard_map/pallas_call | solution.py:419

commit v4 on v3

--- a/solution.py
+++ b/solution.py
@@ -24,7 +24,7 @@
     ne, nz,
     tok_h, gout_h, rt_h, pt_h, wg_h, wu_h, wd_h,
     mixed, gtok, gprob, gw_g, gw_u, gw_d,
-    tok, gout, rt, pt, wg, wu, wd, disp, disp_t, s_buf, r_buf, xg, acc, h_t, h_r, part, tx, rx, own,
+    tok, gout, rt, pt, wg, wu, wd, disp, disp_t, s_in, s_grad, r_in, r_grad, xg, acc, h_t, h_r, part, tx, rx, own,
     sc_all, o_buf, o_home, b_buf, b_home,
     w_sem, a2a_send, a2a_recv, ag_send, ag_recv, rs_send, rs_recv, sc_send, sc_recv,
 ):
@@ -46,11 +46,27 @@
         c.start()
 
     barrier = pltpu.get_barrier_semaphore()
-    def greet(d, carry):
-        pl.semaphore_signal(barrier, inc=1, device_id={"expert": lax.rem(e + d, ne)}, device_id_type=MESH)
-        return carry
-
-    lax.fori_loop(1, ne, greet, 0)
+    def each_peer(act):
+        far_half = ne // 2
+        n = 4 if far_half % 4 == 0 else 1
+
+        def ahead(i, carry):
+            for j in range(n):
+                act(lax.rem(e + far_half + n * i + j, ne))
+            return carry
+
+        def behind(i, carry):
+            for j in range(n):
+                act(lax.rem(e + far_half - 1 - n * i - j, ne))
+            return carry
+
+        lax.fori_loop(0, far_half // n, ahead, 0)
+        lax.fori_loop(0, far_half // n - 1, behind, 0)
+        for d in range(n - 1, 0, -1):
+            act(lax.rem(e + d, ne))
+
+    each_peer(lambda peer: pl.semaphore_signal(
+        barrier, inc=1, device_id={"expert": peer}, device_id_type=MESH))
     near = (1, -1, 2, -2, 3, -3)
     for d in near:
         pl.semaphore_signal(barrier, inc=1, device_id={"mp": z_at(d)}, device_id_type=MESH)
@@ -86,20 +102,15 @@
         return jnp.concatenate(
             [ref[:, 0, 128 * i : 128 * (i + 1)], ref[:, 0, 128 * (i + 1) : 128 * (i + 2)]], axis=0).astype(BF)
 
-    put(s_buf, 0, v_in)
-    put(s_buf, 2, v_grad)
+    put(s_in, 0, v_in)
+    put(s_grad, 0, v_grad)
 
     pl.semaphore_wait(barrier, (ne - 1) + len(near))
 
     def to_all(i, src, dst):
-        def body(d, carry):
-            peer = lax.rem(e + d, ne)
-            pltpu.make_async_remote_copy(
-                src_ref=src.at[peer], dst_ref=dst.at[e], send_sem=a2a_send.at[i], recv_sem=a2a_recv.at[i],
-                device_id={"expert": peer}, device_id_type=MESH).start()
-            return carry
-
-        lax.fori_loop(1, ne, body, 0)
+        each_peer(lambda peer: pltpu.make_async_remote_copy(
+            src_ref=src.at[peer], dst_ref=dst.at[e], send_sem=a2a_send.at[i], recv_sem=a2a_recv.at[i],
+            device_id={"expert": peer}, device_id_type=MESH).start())
         dst[e] = src[e]
 
     def all_of(i, src, dst):
@@ -108,7 +119,8 @@
             send_sem=a2a_send.at[i], recv_sem=a2a_recv.at[i],
             device_id={"expert": lax.rem(e + 1, ne)}, device_id_type=MESH)
 
-    to_all(0, s_buf, r_buf)
+    to_all(0, s_in, r_in)
+    to_all(3, s_grad, r_grad)
 
     t_f = jnp.transpose(d_f)
     t_w = jnp.transpose(d_w)
@@ -121,9 +133,8 @@
 
     for c in loads[4:]:
         c.wait()
-    all_of(0, s_buf, r_buf).wait_recv()
-    for a in range(2):
-        xg[m, a] = take(r_buf, 2 * a)
+    all_of(0, s_in, r_in).wait_recv()
+    xg[m, 0] = take(r_in, 0)
 
     def give(a, o, to):
         blk = z_at(-o)
@@ -181,14 +192,17 @@
         lax.fori_loop(0, n, body, 0)
 
     for a in range(2):
+        if a == 1:
+            all_of(3, s_grad, r_grad).wait_recv()
+            xg[m, 1] = take(r_grad, 0)
         for to in (3, -3, 1, -1):
             give(a, 0, to).start()
-    use_at(0, 0)
+        use_at(a, 0)
     pass3(0)
     use_at(0, 3, -3)
     pass3(1)
     use_many(0, 1, 2)
-    use_at(1, 0, 3, -3)
+    use_at(1, 3, -3)
     pass6(0)
     use_many(0, 2, 4)
     use_at(0, 6, -6)
@@ -291,6 +305,7 @@
     use_many(1, 1, 2)
     use_many(1, 2, 4)
     use_at(1, 6, -6)
+    mid(0, 6, 3, (5, 7, 8))
     use_many(1, 5, 4)
     got(1, far(1))
     use_at(1, far(1))
@@ -299,7 +314,6 @@
     silu = gate * sig
     keep(1, back * up * sig * (1.0 + gate * (1.0 - sig)))
     keep(2, back * silu)
-    mid(0, 6, 3, (5, 7, 8))
     sc_all[m] = jnp.broadcast_to(jnp.sum(silu * up * back, axis=0, keepdims=True), sc_all.shape[1:])
     leaves(1)
     for to in (3, -3, 1, -1):
@@ -316,17 +330,16 @@
     part_of(1, 3)
     for a in range(2):
         own[a] = partial(a, m)
-    weights_from(0, 5)
+    weights_from(0, 6)
+    mid(1, 3, 0, (2, 4, 6))
 
     final(0)
     to_all(1, o_buf, o_home)
-    mid(1, 3, 0, (2, 4, 6))
     for g in (1, -1):
         got_sc(6 * g)
         for to in (7, 5):
             give_sc(6 * g, to * g).start()
     give_sc(6, 8).start()
-    weights_from(5, 16)
 
     for o in (1, -1, 2, -2, 4, -4, 5, -5, 7, -7, 8):
         got_sc(o)
@@ -339,12 +352,15 @@
 
     final(1)
     to_all(2, b_buf, b_home)
+    weights_from(6, 16)
 
     all_of(1, o_buf, o_home).wait_recv()
     out = take(o_home, 0)
     mixed[...] = (dot(disp_t[0], out) + dot(disp_t[1], out)).astype(BF)
 
-    for i, refs in enumerate(((s_buf, r_buf), (o_buf, o_home), (b_buf, b_home))):
+    for i, refs in enumerate(
+        ((s_in, r_in), (o_buf, o_home), (b_buf, b_home), (s_grad, r_grad))
+    ):
         all_of(i, *refs).wait_send()
     for o in range(1, nz):
         for a in range(2):
@@ -397,7 +413,7 @@
             V((nt, width), BF), V((nt, width), BF), V((topk, nt), jnp.int32), V((topk, nt), F32),
             V((f, d), BF), V((f, d), BF), V((f, d), BF),
             V((rows, nt), F32), V((3, nt, rows), BF),
-            V((ne, 1, 512), F32), V((ne, 1, 512), F32),
+            V((ne, 1, 256), F32), V((ne, 1, 256), F32), V((ne, 1, 256), F32), V((ne, 1, 256), F32),
             V((nz, 2, rows, width), BF),
             V((3, f, rows), F32), V((3, f, rows), BF), V((3, rows, f), BF),
             V((2, 2, rows, width), F32),
@@ -405,7 +421,7 @@
             V((2, rows, width), F32),
             V((nz, 8, rows), F32),
             V((ne, 1, 256), F32), V((ne, 1, 256), F32), V((ne, 1, 384), F32), V((ne, 1, 384), F32),
-            dma((7,)), dma((3,)), dma((3,)),
+            dma((7,)), dma((4,)), dma((4,)),
             dma((2, nz)), dma((2, nz)), dma((2, nz)), dma((2, nz)),
             dma((nz,)), dma((nz,)),
         ],

time: 85.5 us -> 85.3 us (level)
  no operation moved by 1% of the time
where the time goes in v4:
time: 85.3 us; the launch traced here: 85.1 us
  Pallas kernels  84.5 us (99%)
    pallas_call x1, Pallas kernels, local(): pl.pallas_call(functools.partial(kernel, ne, nz), out_shape=tuple((pltpu....  83.5 us

profile of v4, /device:TPU:1, one launch (start us, length us, event | category | flops | bytes accessed | tf_op | source)
XLA Modules:
  0.0 85.1 jit_solution(14447730880519543265)
XLA Ops:
  0.6 83.5 %shard_map.118 = (bf16[16,128]{1,0:T(8,128)(2,1)S(1)}, bf16[16,128]{1,0:T(8,128)(2,1)S(1)}, f32[6,16]{1,0:T(8,128)S(1)}, bf16[88,2048]{1,0:T(8,128)(2,1)S(1)}, b...) custom-call(bf16[16,128]{1,0:T(8,128)(2,1)} %tok_h.1, bf16[16,128]{1,0:T(8,128)(2,1)} %gout_h.1, ...), custom_call_target="tpu_custom_call" | custom-call | tf_op jit(solution)/shard_map/pallas_call | solution.py:407
  84.1 1.0 %shard_map.119 = (bf16[16,128]{1,0:T(8,128)(2,1)}, bf16[16,128]{1,0:T(8,128)(2,1)}, f32[6,16]{1,0:T(8,128)}, bf16[88,2048]{1,0:T(8,128)(2,1)}, bf16[88,2048]{1,0:T(8,128)(2,1)}, /*index=5*/bf16[88,2048]{1,0:T(8,128)(2,1)}) custom-call(bf16[16,128]{1,0:T(8,128)(2,1)S(1)} %get-tuple-element.18.refs_0_, bf16[16,128]{1,0:T(8,128)(2,1)S(1)} %get-tuple-element.19.refs_1_, ...), custom_call_target="tpu_custom_call" | custom-call | tf_op jit(solution)/shard_map/pallas_call | solution.py:435
